TPU v7x, 512 devices: a whole 4x4x16 slice. The times are simulated.
512 devices in a mesh: row: 32 (over z, core), col: 16 (over y, x).
Axes of the slice: x: 4, y: 4, z: 16, core: 2. Of those that a mesh axis runs over, the one named last changes fastest.
Arguments:
- tokens: bfloat16 [384, 14336], P('row', 'col'), may hold values from -6 to 6
- w_in: bfloat16 [14336, 40960], P('col', 'row'), may hold values from -0.046875 to 0.046875
- b_in: float32 [40960], P('row'), may hold values from -3 to 3
- w_out: bfloat16 [40960, 14336], P('row', 'col'), may hold values from -0.03125 to 0.03125
- b_out: float32 [14336], P('col'), may hold values from -3 to 3
Outputs:
- block_out: bfloat16 [384, 14336], P('row', 'col')
All inputs are finite; a program needn't handle non-finite values.
Results may differ from a plain program's by a relative error of at most 0.0044.
Values may be sent and summed in bfloat16 or wider, within the bound.
A program may use at most 64 MiB of HBM per device.

v0:
```python
import jax
import jax.numpy as jnp
from jax import lax
from jax.sharding import PartitionSpec as P


def on_device(tokens, w_in, b_in, w_out, b_out):
    partial_in = jnp.dot(
        lax.all_gather(tokens, "row", axis=0, tiled=True), w_in, preferred_element_type=jnp.float32
    )
    shares = lax.psum_scatter(partial_in, "col", scatter_dimension=0, tiled=True)
    hidden_rows = jax.nn.gelu(shares + b_in, approximate=True).astype(jnp.bfloat16)
    partial_out = jnp.dot(
        lax.all_gather(hidden_rows, "col", axis=0, tiled=True),
        w_out,
        preferred_element_type=jnp.float32,
    )
    result = lax.psum_scatter(partial_out, "row", scatter_dimension=0, tiled=True)
    return (result + b_out).astype(jnp.bfloat16)


def solution(mesh):
    return jax.shard_map(
        on_device,
        mesh=mesh,
        in_specs=(P("row", "col"), P("col", "row"), P("row"), P("row", "col"), P("col")),
        out_specs=P("row", "col"),
        check_vma=False,
    )
```

profile of v0, /device:TPU:1, one launch (start us, length us, event | category | flops | bytes accessed | tf_op | source)
XLA Modules:
  0.0 265.7 jit_solution(13135409464923966204)
XLA Ops:
  6.5 0.0 copy-start
  6.5 0.0 reduce-scatter.6.cloned.1.call-start
  6.5 40.4 %all-gather = bf16[32,12,896]{2,1,0:T(8,128)(2,1)S(1)} all-gather(bf16[1,12,896]{2,1,0:T(8,128)(2,1)} %bitcast.9), channel_id=1, replica_groups=mesh['row'=32,'col'=16] {'row'}, dimensions={0}, use_global_device_ids=true | all-gather | bytes 709632 | tf_op jit(solution)/shard_map/all_gather | solution.py:9
  47.0 1.0 reshape.3
  48.0 0.0 copy-done
  48.0 0.0 copy-start.1
  48.0 3.6 %fusion.10 = f32[384,1280]{1,0:T(8,128)} fusion(bf16[384,896]{1,0:T(8,128)(2,1)} %reshape.3, bf16[896,1280]{1,0:T(8,128)(2,1)S(1)} %copy-done), kind=kOutput, calls=%fused_computation.11 | convolution fusion | flops 880803840 | bytes 4947968 | tf_op jit(solution)/shard_map/dot_general | solution.py:8
  51.6 0.0 reduce-scatter.6.cloned.1.call-update
  51.6 83.6 %reduce-scatter.6.cloned.1.call-done = f32[24,1280]{1,0:T(8,128)} async-done(((f32[384,1280]{1,0:T(8,128)}), f32[24,1280]{1,0:T(8,128)}) %reduce-scatter.6.cloned.1.call-update) | async-done | bytes 122896
  135.2 0.0 copy-done.1
  135.2 1.0 fusion.8
  136.1 18.3 %all_gather.7 = bf16[384,1280]{1,0:T(8,128)(2,1)S(1)} all-gather(bf16[24,1280]{1,0:T(8,128)(2,1)S(1)} %fusion.8), channel_id=1, replica_groups=mesh['row'=32,'col'=16] {'col'}, dimensions={0}, use_global_device_ids=true | all-gather | bytes 1044480 | tf_op jit(solution)/shard_map/all_gather | solution.py:14
  154.4 3.9 %fusion.11 = f32[384,896]{1,0:T(8,128)} fusion(bf16[384,1280]{1,0:T(8,128)(2,1)S(1)} %all_gather.7, bf16[1280,896]{1,0:T(8,128)(2,1)} %param.8), kind=kOutput, calls=%fused_computation.12 | convolution fusion | flops 880803840 | bytes 4653056 | tf_op jit(solution)/shard_map/dot_general | solution.py:13
  158.3 0.0 copy-start.2
  158.3 64.4 %fusion = f32[16,896]{1,0:T(8,128)S(1)} fusion(f32[384,896]{1,0:T(8,128)} %fusion.11), kind=kCustom, calls=%all-reduce-scatter | all-reduce-scatter fusion | flops 458753 | bytes 1435648
  222.7 2.4 collective-permute-start
  225.1 1.3 collective-permute-start.1
  226.4 6.3 %collective-permute-start.7 = (f32[12,896]{1,0:T(8,128)S(1)}, f32[12,896]{1,0:T(8,128)S(1)}, u32[]{:S(2)}, u32[]{:S(2)}) collective-permute-start(f32[12,896]{1,0:T(8,128)S(1)} %slice), channel_id=1, source_target_pairs={{0,128},{16,144},{32,160},{48,176},{64,192},{80,208},{96,224},{112... | collective-permute-start | bytes 129032
  232.8 6.8 %collective-permute-start.2 = (f32[16,896]{1,0:T(8,128)S(1)}, f32[16,896]{1,0:T(8,128)S(1)}, u32[]{:S(2)}, u32[]{:S(2)}) collective-permute-start(f32[16,896]{1,0:T(8,128)S(1)} %fusion), channel_id=1, source_target_pairs={{0,48},{16,64},{32,80},{48,96},{64,112},{80,128},{96,144},{112,160... | collective-permute-start | bytes 172040
  239.6 4.5 %collective-permute-start.3 = (f32[16,896]{1,0:T(8,128)S(1)}, f32[16,896]{1,0:T(8,128)S(1)}, u32[]{:S(2)}, u32[]{:S(2)}) collective-permute-start(f32[16,896]{1,0:T(8,128)S(1)} %fusion), channel_id=1, source_target_pairs={{0,64},{16,80},{32,96},{48,112},{64,128},{80,144},{96,160},{112,17... | collective-permute-start | bytes 172040
  244.1 0.0 collective-permute-done.7
  244.1 5.5 %collective-permute-start.4 = (f32[16,896]{1,0:T(8,128)S(1)}, f32[16,896]{1,0:T(8,128)S(1)}, u32[]{:S(2)}, u32[]{:S(2)}) collective-permute-start(f32[16,896]{1,0:T(8,128)S(1)} %fusion), channel_id=1, source_target_pairs={{0,80},{16,96},{32,112},{48,128},{64,144},{80,160},{96,176},{112,1... | collective-permute-start | bytes 172040
  249.6 0.0 collective-permute-done
  249.6 1.7 collective-permute-start.5
  251.3 0.0 collective-permute-done.1
  251.3 3.8 %collective-permute-start.6 = (f32[16,896]{1,0:T(8,128)S(1)}, f32[16,896]{1,0:T(8,128)S(1)}, u32[]{:S(2)}, u32[]{:S(2)}) collective-permute-start(f32[16,896]{1,0:T(8,128)S(1)} %fusion), channel_id=1, source_target_pairs={{0,112},{16,128},{32,144},{48,160},{64,176},{80,192},{96,208},{112... | collective-permute-start | bytes 172040
  255.1 1.3 dynamic-slice.6
  257.1 0.0 collective-permute-done.2
  257.1 0.0 collective-permute-done.3
  257.1 0.0 collective-permute-done.4
  257.1 0.0 collective-permute-done.5
  257.1 0.0 collective-permute-done.6
  257.1 1.1 concatenate
  258.2 0.0 copy-done.2
  258.2 0.6 fusion.9
  (1 shorter events, 0.0 us)
Async XLA Ops:
  6.5 41.4 %copy-start = (bf16[896,1280]{1,0:T(8,128)(2,1)S(1)}, bf16[896,1280]{1,0:T(8,128)(2,1)}, u32[]{:S(2)}) copy-start(bf16[896,1280]{1,0:T(8,128)(2,1)} %param.6) | copy-start | bytes 6881284
  6.5 128.6 %reduce-scatter.6.cloned.1.call-start = ((), (), s32[]{:S(2)}) async-start(), calls=%async_computation.1 | async-start | bytes 2088960
  48.0 87.2 %copy-start.1 = (f32[1280]{0:T(1024)S(1)}, f32[1280]{0:T(1024)}, u32[]{:S(2)}) copy-start(f32[1280]{0:T(1024)} %param.7) | copy-start | bytes 15364
  158.3 99.9 %copy-start.2 = (f32[896]{0:T(1024)S(1)}, f32[896]{0:T(1024)}, u32[]{:S(2)}) copy-start(f32[896]{0:T(1024)} %param.9) | copy-start | bytes 10756
  222.7 26.9 %collective-permute-start = (f32[16,896]{1,0:T(8,128)S(1)}, f32[16,896]{1,0:T(8,128)S(1)}, u32[]{:S(2)}, u32[]{:S(2)}) collective-permute-start(f32[16,896]{1,0:T(8,128)S(1)} %fusion), channel_id=1, source_target_pairs={{0,16},{16,32},{32,48},{48,64},{64,80},{80,96},{96,112},{112,128},... | collective-permute-start | bytes 172040
  225.1 26.2 %collective-permute-start.1 = (f32[16,896]{1,0:T(8,128)S(1)}, f32[16,896]{1,0:T(8,128)S(1)}, u32[]{:S(2)}, u32[]{:S(2)}) collective-permute-start(f32[16,896]{1,0:T(8,128)S(1)} %fusion), channel_id=1, source_target_pairs={{0,32},{16,48},{32,64},{48,80},{64,96},{80,112},{96,128},{112,144}... | collective-permute-start | bytes 172040
  226.4 17.7 %collective-permute-start.7 = (f32[12,896]{1,0:T(8,128)S(1)}, f32[12,896]{1,0:T(8,128)S(1)}, u32[]{:S(2)}, u32[]{:S(2)}) collective-permute-start(f32[12,896]{1,0:T(8,128)S(1)} %slice), channel_id=1, source_target_pairs={{0,128},{16,144},{32,160},{48,176},{64,192},{80,208},{96,224},{112... | collective-permute-start | bytes 129032
  232.8 24.3 %collective-permute-start.2 = (f32[16,896]{1,0:T(8,128)S(1)}, f32[16,896]{1,0:T(8,128)S(1)}, u32[]{:S(2)}, u32[]{:S(2)}) collective-permute-start(f32[16,896]{1,0:T(8,128)S(1)} %fusion), channel_id=1, source_target_pairs={{0,48},{16,64},{32,80},{48,96},{64,112},{80,128},{96,144},{112,160... | collective-permute-start | bytes 172040
  239.6 17.5 %collective-permute-start.3 = (f32[16,896]{1,0:T(8,128)S(1)}, f32[16,896]{1,0:T(8,128)S(1)}, u32[]{:S(2)}, u32[]{:S(2)}) collective-permute-start(f32[16,896]{1,0:T(8,128)S(1)} %fusion), channel_id=1, source_target_pairs={{0,64},{16,80},{32,96},{48,112},{64,128},{80,144},{96,160},{112,17... | collective-permute-start | bytes 172040
  244.1 13.0 %collective-permute-start.4 = (f32[16,896]{1,0:T(8,128)S(1)}, f32[16,896]{1,0:T(8,128)S(1)}, u32[]{:S(2)}, u32[]{:S(2)}) collective-permute-start(f32[16,896]{1,0:T(8,128)S(1)} %fusion), channel_id=1, source_target_pairs={{0,80},{16,96},{32,112},{48,128},{64,144},{80,160},{96,176},{112,1... | collective-permute-start | bytes 172040
  249.6 7.5 %collective-permute-start.5 = (f32[16,896]{1,0:T(8,128)S(1)}, f32[16,896]{1,0:T(8,128)S(1)}, u32[]{:S(2)}, u32[]{:S(2)}) collective-permute-start(f32[16,896]{1,0:T(8,128)S(1)} %fusion), channel_id=1, source_target_pairs={{0,96},{16,112},{32,128},{48,144},{64,160},{80,176},{96,192},{112,... | collective-permute-start | bytes 172040
  251.3 5.8 %collective-permute-start.6 = (f32[16,896]{1,0:T(8,128)S(1)}, f32[16,896]{1,0:T(8,128)S(1)}, u32[]{:S(2)}, u32[]{:S(2)}) collective-permute-start(f32[16,896]{1,0:T(8,128)S(1)} %fusion), channel_id=1, source_target_pairs={{0,112},{16,128},{32,144},{48,160},{64,176},{80,192},{96,208},{112... | collective-permute-start | bytes 172040
Sparse Core Ops, SparseCore 0:
  51.7 83.4 reduce-scatter.5
where the time goes:
time: 266 us
  blocking collectives  123 us (46%)
  waiting for transfers between devices  83.6 us (31%)
  starting transfers between devices  32.4 us (12%)
  between operations  14.2 us (5%)
  matrix products  7.53 us (3%)
  local copies, waits for them, and re-layouts  3.37 us (1%)
    unnamed x10, waiting for transfers between devices  83.6 us
    unnamed x1, blocking collectives  64.4 us
    all_gather x1, blocking collectives, on_device(): lax.all_gather(tokens, 'row', axis=0, tiled=True)  40.4 us
    unnamed x9, starting transfers between devices  32.4 us
    all_gather x1, blocking collectives, on_device(): lax.all_gather(hidden_rows, 'col', axis=0, tiled=True)  18.3 us
  transfers between devices with their start and end apart: 9, of which 1 were waited for; matrix products, arithmetic and copies ran while one was open for 0% of the time, Pallas kernels for 0%

commit v1 on v0

v1 whole, which is shorter than its diff:
```python
import functools

import jax
import jax.numpy as jnp
from jax import lax
from jax.experimental import pallas as pl
from jax.experimental.pallas import tpu as pltpu
from jax.sharding import PartitionSpec as P

BF16 = jnp.bfloat16
F32 = jnp.float32
PARENT = {1: 0, 2: 0, 4: 0, 3: 2, 5: 4, 6: 4, 8: 4, 7: 6}
BASE = {1: 1, 2: 3, 4: 5, 3: 7, 5: 9, 6: 11, 7: 13, 8: 15}
PLANE = [(dy, dx) for dy in (2, 1, 3, 0) for dx in (2, 1, 3, 0) if (dy, dx) != (0, 0)]
GROUPS = 3
A_CUTS = (0, 6, 12, 16)
D_CUTS = (0, 5, 10, 16)


def slot(side, m):
    return BASE[m] + side


def kernel(
    tok_ref, win_ref, bin_ref, wout_ref, bout_ref, o_ref,
    win, wout, ta, xs, pf, pb, rb, hid, po, ss, sr, zs, zr,
    wsem, a_send, a_recv, as_send, as_recv, b_send, b_recv, c_send, c_recv,
    ds_send, ds_recv, d_send, d_recv,
):
    row, col = lax.axis_index("row"), lax.axis_index("col")
    z, c = row // 2, row % 2
    y, x = col // 4, col % 4
    half = pb.shape[-1]
    s8 = 1 - 2 * c

    def z_peer(dz):
        return {"row": lax.rem(z + dz + 16, 16) * 2 + c, "col": col}

    def plane_col(dy, dx):
        return lax.rem(y + dy + 4, 4) * 4 + lax.rem(x + dx + 4, 4)

    def plane_peer(dy, dx):
        return {"row": row, "col": plane_col(dy, dx)}

    sibling = {"row": z * 2 + (1 - c), "col": col}

    def remote(src, dst, send, recv, peer):
        return pltpu.make_async_remote_copy(
            src_ref=src, dst_ref=dst, send_sem=send, recv_sem=recv,
            device_id=peer, device_id_type=pl.DeviceIdType.MESH,
        )

    sent = []

    def start(copy):
        copy.start()
        sent.append(copy)

    load_in = pltpu.make_async_copy(win_ref, win, wsem.at[0])
    load_out = pltpu.make_async_copy(wout_ref, wout, wsem.at[1])
    load_in.start()
    load_out.start()

    barrier = pltpu.get_barrier_semaphore()
    peers = [z_peer(dz) for dz in (4, -4, 2, -2, 1, -1)]
    peers += [plane_peer(dy, dx) for dy, dx in PLANE] + [sibling]
    for peer in peers:
        pl.semaphore_signal(barrier, inc=1, device_id=peer, device_id_type=pl.DeviceIdType.MESH)

    own = tok_ref[...].astype(F32)
    tail, none = own[8:12], jnp.zeros((4, own.shape[1]), F32)
    tail = jnp.where(
        c == 0, jnp.concatenate([tail, none], axis=0), jnp.concatenate([none, tail], axis=0)
    )
    ta[c, 0] = jnp.concatenate([own[0:8], tail], axis=0).astype(BF16)
    pl.semaphore_wait(barrier, len(peers))

    def a_copy(side, m, at):
        sign = 1 - 2 * side
        dz = -sign * (m - PARENT[m])
        place = slot(side, m)
        return remote(ta.at[c, at], ta.at[c, place], a_send.at[side, m], a_recv.at[side, m], z_peer(dz))

    def a_copy8():
        return remote(ta.at[c, slot(0, 4) + c], ta.at[c, 15], a_send.at[0, 8], a_recv.at[0, 8], z_peer(-4 * s8))

    def a_wait(side, m):
        a_copy(side, m, 0).wait_recv()

    def a_sibling(g):
        part = pl.ds(A_CUTS[g], A_CUTS[g + 1] - A_CUTS[g])
        return remote(ta.at[c, part], ta.at[c, part], as_send.at[g], as_recv.at[g], sibling)

    def a_sibling_wait(g):
        part = pl.ds(A_CUTS[g], A_CUTS[g + 1] - A_CUTS[g])
        remote(ta.at[1 - c, part], ta.at[1 - c, part], as_send.at[g], as_recv.at[g], sibling).wait_recv()

    def assemble(g):
        for k in range(A_CUTS[g], A_CUTS[g + 1], 2):
            rows = []
            for i in (k, k + 1):
                first, second = ta[0, i].astype(F32), ta[1, i].astype(F32)
                rows += [first[0:8], second[0:8], first[8:16] + second[8:16]]
            xs[24 * k : 24 * k + 48, :] = jnp.concatenate(rows, axis=0).astype(BF16)

    def project_in(g):
        lhs = xs[128 * g : 128 * g + 128, :]

        @pl.loop(0, 2)
        def _(h):
            cols = pl.ds(pl.multiple_of(h * half, 128), half)
            part = jnp.dot(lhs, win[:, cols], preferred_element_type=F32).reshape(8, 16, half)
            pf[g, :, h] = part
            pb[g, :, h] = part.astype(BF16)

    def b_copy(g, dy, dx):
        there = plane_col(dy, dx)
        d = dy * 4 + dx
        return remote(
            pb.at[g, there // 2, there % 2], rb.at[g, d], b_send.at[g, d], b_recv.at[g, d], plane_peer(dy, dx)
        )

    def b_start(g):
        for dy, dx in PLANE:
            start(b_copy(g, dy, dx))

    def b_finish(g):
        total = pf[g, col // 2, col % 2]
        for dy, dx in reversed(PLANE):
            b_copy(g, dy, dx).wait_recv()
            total += rb[g, dy * 4 + dx].astype(F32)
        v = total + bin_ref[:, pl.ds(pl.multiple_of((col % 2) * half, 128), half)]
        v = 0.5 * v * (1.0 + jnp.tanh(0.7978845608 * (v + 0.044715 * (v * v * v))))
        hid[g, col // 2, col % 2] = v.astype(BF16)

    def c_start(g):
        block = hid.at[g, col // 2, col % 2]
        for dy, dx in PLANE:
            d = dy * 4 + dx
            start(remote(block, block, c_send.at[g, d], c_recv.at[g, d], plane_peer(dy, dx)))

    def c_wait(g):
        for dy, dx in reversed(PLANE):
            d = dy * 4 + dx
            there = plane_col(-dy, -dx)
            block = hid.at[g, there // 2, there % 2]
            remote(block, block, c_send.at[g, d], c_recv.at[g, d], plane_peer(-dy, -dx)).wait_recv()

    def project_out(g):
        total = jnp.zeros((128, po.shape[1]), F32)
        for h in range(2):
            lhs = hid[g, :, h].reshape(128, half)
            total += jnp.dot(lhs, wout[h * half : (h + 1) * half, :], preferred_element_type=F32)
        po[128 * g : 128 * g + 128, :] = total

    def share(k, core):
        first = po[pl.ds(pl.multiple_of(24 * k + 8 * core, 8), 8), :]
        return jnp.concatenate([first, po[pl.ds(pl.multiple_of(24 * k + 16, 8), 8), :]], axis=0)

    def d_sibling(g):
        part = pl.ds(D_CUTS[g], D_CUTS[g + 1] - D_CUTS[g])
        return remote(ss.at[part], sr.at[part], ds_send.at[g], ds_recv.at[g], sibling)

    def d_sibling_start(g):
        for k in range(D_CUTS[g], D_CUTS[g + 1]):
            ss[k] = share(k, 1 - c).astype(BF16)
        start(d_sibling(g))

    def chip(k):
        return share(k, c) + sr[k].astype(F32)

    def d_copy(side, m):
        sign = 1 - 2 * side
        place = BASE[m] + side
        return remote(
            zs.at[place], zr.at[place], d_send.at[side, m], d_recv.at[side, m], z_peer(sign * (m - PARENT[m]))
        )

    def d_copy8():
        return remote(zs.at[15], zr.at[15], d_send.at[0, 8], d_recv.at[0, 8], z_peer(4 * s8))

    def d_send_on(side, m, below=()):
        place = BASE[m] + side
        total = chip(place)
        for n in below:
            if n == 8:
                d_copy8().wait_recv()
                total += zr[15].astype(F32)
            else:
                d_copy(side, n).wait_recv()
                total += zr[BASE[n] + side].astype(F32)
        zs[place] = total.astype(BF16)
        start(d_copy(side, m))

    for m in (4, 2, 1):
        for side in (0, 1):
            start(a_copy(side, m, 0))
    for m in (2,):
        for side in (0, 1):
            a_wait(side, m)
            start(a_copy(side, 3, slot(side, 2)))
    for side in (0, 1):
        a_wait(side, 1)
    for side in (0, 1):
        a_wait(side, 4)
        start(a_copy(side, 6, slot(side, 4)))
        start(a_copy(side, 5, slot(side, 4)))
    start(a_copy8())
    start(a_sibling(0))
    a_sibling_wait(0)
    assemble(0)
    load_in.wait()
    project_in(0)
    b_start(0)
    for side in (0, 1):
        a_wait(side, 6)
        start(a_copy(side, 7, slot(side, 6)))
    for side in (0, 1):
        a_wait(side, 5)
        a_wait(side, 3)
    start(a_sibling(1))
    a_sibling_wait(1)
    assemble(1)
    project_in(1)
    b_start(1)
    for side in (0, 1):
        a_wait(side, 7)
    a_copy8().wait_recv()
    start(a_sibling(2))
    b_finish(0)
    c_start(0)
    a_sibling_wait(2)
    assemble(2)
    project_in(2)
    b_start(2)
    b_finish(1)
    c_start(1)
    load_out.wait()
    c_wait(0)
    project_out(0)
    d_sibling_start(0)
    b_finish(2)
    c_start(2)
    d_sibling(0).wait_recv()
    for side in (0, 1):
        d_send_on(side, 1)
    c_wait(1)
    project_out(1)
    d_sibling_start(1)
    d_sibling(1).wait_recv()
    for side in (0, 1):
        d_send_on(side, 3)
    d_send_on(0, 5)
    for side in (0, 1):
        d_send_on(side, 2, (3,))
    c_wait(2)
    project_out(2)
    d_sibling_start(2)
    d_sibling(2).wait_recv()
    for side in (0, 1):
        d_send_on(side, 7)
    zs[15] = chip(15).astype(BF16)
    start(d_copy8())
    d_send_on(1, 5)
    for side in (0, 1):
        d_send_on(side, 6, (7,))
    d_send_on(1 - c, 4, (5, 6))
    d_send_on(c, 4, (5, 6, 8))
    total = chip(0)
    for m in (1, 2, 4):
        for side in (0, 1):
            d_copy(side, m).wait_recv()
            total += zr[BASE[m] + side].astype(F32)
    last = jnp.where(c == 0, total[8:12], total[12:16])
    out = jnp.concatenate([total[0:8], last], axis=0) + bout_ref[...]
    o_ref[...] = out.astype(BF16)
    for copy in sent:
        copy.wait_send()


def on_device(tokens, w_in, b_in, w_out, b_out):
    width, hidden = w_in.shape
    half = hidden // 2
    vmem = pl.BlockSpec(memory_space=pltpu.VMEM)
    hbm = pl.BlockSpec(memory_space=pl.ANY)
    dma = pltpu.SemaphoreType.DMA
    return pl.pallas_call(
        kernel,
        out_shape=jax.ShapeDtypeStruct(tokens.shape, BF16),
        in_specs=[vmem, hbm, vmem, hbm, vmem],
        out_specs=vmem,
        scratch_shapes=[
            pltpu.VMEM((width, hidden), BF16),
            pltpu.VMEM((hidden, width), BF16),
            pltpu.VMEM((2, 16, 16, width), BF16),
            pltpu.VMEM((384, width), BF16),
            pltpu.VMEM((GROUPS, 8, 2, 16, half), F32),
            pltpu.VMEM((GROUPS, 8, 2, 16, half), BF16),
            pltpu.VMEM((GROUPS, 16, 16, half), BF16),
            pltpu.VMEM((GROUPS, 8, 2, 16, half), BF16),
            pltpu.VMEM((384, width), F32),
            pltpu.VMEM((16, 16, width), BF16),
            pltpu.VMEM((16, 16, width), BF16),
            pltpu.VMEM((16, 16, width), BF16),
            pltpu.VMEM((16, 16, width), BF16),
            dma((2,)),
            dma((2, 9)), dma((2, 9)),
            dma((GROUPS,)), dma((GROUPS,)),
            dma((GROUPS, 16)), dma((GROUPS, 16)),
            dma((GROUPS, 16)), dma((GROUPS, 16)),
            dma((GROUPS,)), dma((GROUPS,)),
            dma((2, 9)), dma((2, 9)),
        ],
        compiler_params=pltpu.CompilerParams(
            collective_id=0, has_side_effects=True, vmem_limit_bytes=40 * 2**20
        ),
        cost_estimate=pl.CostEstimate(
            flops=4 * 384 * width * hidden, bytes_accessed=4 * width * hidden, transcendentals=384 * hidden // 16
        ),
    )(tokens, w_in, b_in.reshape(1, -1), w_out, b_out.reshape(1, -1))


def solution(mesh):
    return jax.shard_map(
        on_device,
        mesh=mesh,
        in_specs=(P("row", "col"), P("col", "row"), P("row"), P("row", "col"), P("col")),
        out_specs=P("row", "col"),
        check_vma=False,
    )
```

time: 266 us -> 74.6 us (0.28)
  the two profiles are of different devices: /device:TPU:1 before, /device:TPU:6 now
where the time goes in v1:
time: 74.6 us; the launch traced here: 74.3 us
  Pallas kernels  68.2 us (91%)
  local copies, waits for them, and re-layouts  6.04 us (8%)
    pallas_call x1, Pallas kernels, on_device(): pl.pallas_call(kernel, out_shape=jax.ShapeDtypeStruct(tokens.shape, BF16)...  68.2 us
    unnamed x7, local copies, waits for them, and re-layouts  4.65 us

profile of v1, /device:TPU:6, one launch (start us, length us, event | category | flops | bytes accessed | tf_op | source)
XLA Modules:
  0.0 74.3 jit_solution(17507179430775486347)
XLA Ops:
  0.0 0.7 reshape.7.bout_ref
  0.7 0.7 reshape.6.bin_ref
  1.4 0.0 copy-start
  1.4 1.6 %copy-done = bf16[896,1280]{1,0:T(8,128)(2,1)S(1)} copy-done((bf16[896,1280]{1,0:T(8,128)(2,1)S(1)}, bf16[896,1280]{1,0:T(8,128)(2,1)}, u32[]{:S(2)}) %copy-start) | copy-done | bytes 2293784
  3.0 0.0 copy-start.1
  3.0 1.6 %copy-done.1 = bf16[1280,896]{1,0:T(8,128)(2,1)S(1)} copy-done((bf16[1280,896]{1,0:T(8,128)(2,1)S(1)}, bf16[1280,896]{1,0:T(8,128)(2,1)}, u32[]{:S(2)}) %copy-start.1) | copy-done | bytes 2293784
  4.7 0.0 copy-start.2
  4.7 0.7 %copy-done.2 = bf16[12,896]{1,0:T(8,128)(2,1)S(1)} copy-done((bf16[12,896]{1,0:T(8,128)(2,1)S(1)}, bf16[12,896]{1,0:T(8,128)(2,1)}, u32[]{:S(2)}) %copy-start.2) | copy-done | bytes 21528
  5.4 68.2 %shard_map.55 = bf16[12,896]{1,0:T(8,128)(2,1)S(1)} custom-call(bf16[12,896]{1,0:T(8,128)(2,1)S(1)} %copy-done.2, bf16[896,1280]{1,0:T(8,128)(2,1)S(1)} %copy-done, f32[1,1280]{1,0:T(1,128)S(1)} %reshape.6.bin_ref, bf16[1280,896]{1,0:T(8,128)(2,1)S(1)} %copy-done.1, f32[1,896]{1,0:T(1,128)S(1)} %reshape.7.bout_ref), custom_call_target="tpu_custom_call" | custom-call | flops 1761607680 | bytes 4587520 | tf_op jit(solution)/shard_map/pallas_call | solution.py:287
  73.7 0.6 copy.7
Async XLA Ops:
  1.4 1.6 %copy-start = (bf16[896,1280]{1,0:T(8,128)(2,1)S(1)}, bf16[896,1280]{1,0:T(8,128)(2,1)}, u32[]{:S(2)}) copy-start(bf16[896,1280]{1,0:T(8,128)(2,1)} %win_ref.1) | copy-start | bytes 6881284
  3.0 1.6 %copy-start.1 = (bf16[1280,896]{1,0:T(8,128)(2,1)S(1)}, bf16[1280,896]{1,0:T(8,128)(2,1)}, u32[]{:S(2)}) copy-start(bf16[1280,896]{1,0:T(8,128)(2,1)} %wout_ref.1) | copy-start | bytes 6881284
  4.7 0.7 %copy-start.2 = (bf16[12,896]{1,0:T(8,128)(2,1)S(1)}, bf16[12,896]{1,0:T(8,128)(2,1)}, u32[]{:S(2)}) copy-start(bf16[12,896]{1,0:T(8,128)(2,1)} %tok_ref.1) | copy-start | bytes 64516

commit v2 on v1

v2 whole, which is shorter than its diff:
```python
import functools

import jax
import jax.numpy as jnp
from jax import lax
from jax.experimental import pallas as pl
from jax.experimental.pallas import tpu as pltpu
from jax.sharding import PartitionSpec as P

BF16 = jnp.bfloat16
F32 = jnp.float32
PARENT = {1: 0, 2: 0, 5: 0, 3: 2, 4: 5, 6: 5, 7: 5, 8: 5}
OWN = 15
PLANE = [(dy, dx) for dy in (2, 1, 3, 0) for dx in (2, 1, 3, 0) if (dy, dx) != (0, 0)]
GROUPS = 3
A_CUTS = (0, 6, 10, 16)
D_CUTS = (0, 5, 10, 16)


def slot(side, m):
    if m == 3:
        return 10 - side
    return {8: 0, 7: 1, 6: 3, 4: 5, 5: 7, 2: 11, 1: 13}[m] + side


def parent_out(side, m):
    return 0 if m == 3 and side == 0 else PARENT[m]


def kernel(
    tok_hbm, win_ref, bin_hbm, wout_ref, bout_hbm, o_ref,
    tok, win, b_in, wout, b_out, ta, xs, pf, pb, rb, hid, po, ss, sr, zs, zr,
    wsem, a_send, a_recv, as_send, as_recv, b_send, b_recv, c_send, c_recv,
    ds_send, ds_recv, d_send, d_recv,
):
    row, col = lax.axis_index("row"), lax.axis_index("col")
    z, c = row // 2, row % 2
    y, x = col // 4, col % 4
    half = pb.shape[-1]
    s8 = 1 - 2 * c

    def z_peer(dz):
        return {"row": lax.rem(z + dz + 16, 16) * 2 + c, "col": col}

    def plane_col(dy, dx):
        return lax.rem(y + dy + 4, 4) * 4 + lax.rem(x + dx + 4, 4)

    def plane_peer(dy, dx):
        return {"row": row, "col": plane_col(dy, dx)}

    sibling = {"row": z * 2 + (1 - c), "col": col}

    def remote(src, dst, send, recv, peer):
        return pltpu.make_async_remote_copy(
            src_ref=src, dst_ref=dst, send_sem=send, recv_sem=recv,
            device_id=peer, device_id_type=pl.DeviceIdType.MESH,
        )

    def start(copy):
        copy.start()

    def all_of(block, send, recv):
        return remote(block, block, send, recv, sibling)

    load_tok = pltpu.make_async_copy(tok_hbm, tok, wsem.at[2])
    load_tok.start()

    barrier = pltpu.get_barrier_semaphore()
    peers = [z_peer(dz) for dz in (5, -5, 3, -3, 2, -2, 1, -1)]
    peers += [plane_peer(dy, dx) for dy, dx in PLANE] + [sibling]
    for peer in peers:
        pl.semaphore_signal(barrier, inc=1, device_id=peer, device_id_type=pl.DeviceIdType.MESH)
    load_in = pltpu.make_async_copy(win_ref, win, wsem.at[0])
    load_out = pltpu.make_async_copy(wout_ref, wout, wsem.at[1])
    load_b_in = pltpu.make_async_copy(bin_hbm, b_in, wsem.at[3])
    load_b_out = pltpu.make_async_copy(bout_hbm, b_out, wsem.at[4])
    for load in (load_in, load_out, load_b_in, load_b_out):
        load.start()
    load_tok.wait()

    own = tok[...].astype(F32)
    tail, none = own[8:12], jnp.zeros((4, own.shape[1]), F32)
    tail = jnp.where(
        c == 0, jnp.concatenate([tail, none], axis=0), jnp.concatenate([none, tail], axis=0)
    )
    ta[c, OWN] = jnp.concatenate([own[0:8], tail], axis=0).astype(BF16)
    pl.semaphore_wait(barrier, len(peers))

    def a_copy(side, m, at):
        sign = 1 - 2 * side
        dz = -sign * (m - PARENT[m])
        place = slot(side, m)
        return remote(ta.at[c, at], ta.at[c, place], a_send.at[0], a_recv.at[side, m], z_peer(dz))

    def a_copy8():
        return remote(ta.at[c, slot(0, 5) + c], ta.at[c, 0], a_send.at[0], a_recv.at[0, 8], z_peer(-3 * s8))

    def a_wait(side, m):
        a_copy(side, m, 0).wait_recv()

    def a_sibling(g, place):
        start(remote(ta.at[c, place], ta.at[c, place], as_send.at[0], as_recv.at[g], sibling))

    def a_sibling_wait(g):
        part = pl.ds(A_CUTS[g], A_CUTS[g + 1] - A_CUTS[g])
        all_of(ta.at[1 - c, part], as_send.at[0], as_recv.at[g]).wait_recv()

    def a_take(side, m):
        a_wait(side, m)
        place = slot(side, m)
        a_sibling(sum(place >= cut for cut in A_CUTS[1:]), place)

    def a_sent():
        all_of(ta.at[c, pl.ds(0, 15)], a_send.at[0], as_recv.at[0]).wait_send()
        all_of(ta.at[c], as_send.at[0], as_recv.at[0]).wait_send()

    def assemble(g):
        for k in range(A_CUTS[g], A_CUTS[g + 1], 2):
            rows = []
            for i in (k, k + 1):
                first, second = ta[0, i].astype(F32), ta[1, i].astype(F32)
                rows += [first[0:8], second[0:8], first[8:16] + second[8:16]]
            xs[24 * k : 24 * k + 48, :] = jnp.concatenate(rows, axis=0).astype(BF16)

    def project_in(g):
        lhs = xs[128 * g : 128 * g + 128, :]

        @pl.loop(0, 2)
        def _(h):
            cols = pl.ds(pl.multiple_of(h * half, 128), half)
            part = jnp.dot(lhs, win[:, cols], preferred_element_type=F32).reshape(8, 16, half)
            pf[g, :, h] = part
            pb[g, :, h] = part.astype(BF16)

    def b_copy(g, dy, dx):
        there = plane_col(dy, dx)
        d = dy * 4 + dx
        return remote(
            pb.at[g, there // 2, there % 2], rb.at[g, d], b_send.at[g], b_recv.at[g], plane_peer(dy, dx)
        )

    def b_start(g):
        for dy, dx in PLANE:
            start(b_copy(g, dy, dx))

    def b_finish(g):
        total = pf[g, col // 2, col % 2]
        blocks = all_of(rb.at[g, pl.ds(1, 15)], b_send.at[g], b_recv.at[g])
        blocks.wait_recv()
        for dy, dx in PLANE:
            total += rb[g, dy * 4 + dx].astype(F32)
        v = total + b_in[pl.ds(pl.multiple_of((col % 2) * half, 128), half)].reshape(1, half)
        v = 0.5 * v * (1.0 + jnp.tanh(0.7978845608 * (v + 0.044715 * (v * v * v))))
        hid[g, col // 2, col % 2] = v.astype(BF16)

    def c_start(g):
        block = hid.at[g, col // 2, col % 2]
        for dy, dx in PLANE:
            start(remote(block, block, c_send.at[g], c_recv.at[g], plane_peer(dy, dx)))

    def c_wait(g):
        all_of(rb.at[g, pl.ds(1, 15)], c_send.at[g], c_recv.at[g]).wait_recv()

    def plane_sent(g):
        all_of(rb.at[g, pl.ds(1, 15)], b_send.at[g], b_recv.at[g]).wait_send()
        all_of(rb.at[g, pl.ds(1, 15)], c_send.at[g], c_recv.at[g]).wait_send()

    def project_out(g):
        total = jnp.zeros((128, po.shape[1]), F32)
        for h in range(2):
            lhs = hid[g, :, h].reshape(128, half)
            total += jnp.dot(lhs, wout[h * half : (h + 1) * half, :], preferred_element_type=F32)
        po[128 * g : 128 * g + 128, :] = total

    def share(k, core):
        first = po[pl.ds(pl.multiple_of(24 * k + 8 * core, 8), 8), :]
        return jnp.concatenate([first, po[pl.ds(pl.multiple_of(24 * k + 16, 8), 8), :]], axis=0)

    def d_sibling(g):
        part = pl.ds(D_CUTS[g], D_CUTS[g + 1] - D_CUTS[g])
        return remote(ss.at[part], sr.at[part], ds_send.at[0], ds_recv.at[g], sibling)

    def d_sibling_start(g):
        for k in range(D_CUTS[g], D_CUTS[g + 1]):
            ss[k] = share(k, 1 - c).astype(BF16)
        start(d_sibling(g))

    def chip(k):
        return share(k, c) + sr[k].astype(F32)

    def d_copy(side, m):
        dz = (1 - 2 * side) * (m - parent_out(side, m))
        place = slot(side, m)
        return remote(zs.at[place], zr.at[place], d_send.at[0], d_recv.at[side, m], z_peer(dz))

    def d_copy8():
        return remote(zs.at[0], zr.at[0], d_send.at[0], d_recv.at[0, 8], z_peer(3 * s8))

    def d_sent():
        all_of(sr, ds_send.at[0], ds_recv.at[0]).wait_send()
        all_of(zr.at[pl.ds(0, 15)], d_send.at[0], ds_recv.at[0]).wait_send()

    def d_send_on(side, m, below=()):
        place = slot(side, m)
        total = chip(place)
        for n in below:
            if n == 8:
                d_copy8().wait_recv()
                total += zr[0].astype(F32)
            else:
                d_copy(side, n).wait_recv()
                total += zr[slot(side, n)].astype(F32)
        zs[place] = total.astype(BF16)
        start(d_copy(side, m))

    for m in (5, 2, 1):
        for side in (0, 1):
            start(a_copy(side, m, OWN))
    a_sibling(2, OWN)
    for side in (0, 1):
        a_take(side, 2)
        start(a_copy(side, 3, slot(side, 2)))
    for side in (0, 1):
        a_take(side, 1)
    for side in (0, 1):
        a_take(side, 5)
        for m in (7, 6, 4):
            start(a_copy(side, m, slot(side, 5)))
    start(a_copy8())
    a_take(0, 3)
    load_in.wait()
    load_b_in.wait()
    load_b_out.wait()
    a_sibling_wait(2)
    assemble(2)
    project_in(2)
    b_start(2)
    for m in (6, 7):
        for side in (0, 1):
            a_take(side, m)
    a_copy8().wait_recv()
    a_sibling(0, 0)
    a_take(0, 4)
    a_take(1, 4)
    a_take(1, 3)
    a_sibling_wait(0)
    assemble(0)
    project_in(0)
    b_start(0)
    a_sibling_wait(1)
    assemble(1)
    project_in(1)
    b_start(1)
    load_out.wait()
    b_finish(2)
    b_finish(0)
    c_start(0)
    a_sent()
    b_finish(1)
    c_start(1)
    c_start(2)
    c_wait(0)
    project_out(0)
    d_sibling_start(0)
    d_sibling(0).wait_recv()
    zs[0] = chip(0).astype(BF16)
    start(d_copy8())
    for m in (7, 6):
        for side in (0, 1):
            d_send_on(side, m)
    c_wait(1)
    project_out(1)
    d_sibling_start(1)
    d_sibling(1).wait_recv()
    for side in (0, 1):
        d_send_on(side, 4)
    d_send_on(1, 3)
    c_wait(2)
    project_out(2)
    d_sibling_start(2)
    d_send_on(1 - c, 5, (4, 6, 7))
    d_send_on(c, 5, (4, 6, 7, 8))
    d_sibling(2).wait_recv()
    d_send_on(0, 3)
    d_send_on(0, 2)
    d_send_on(1, 2, (3,))
    for side in (0, 1):
        d_send_on(side, 1)
    for g in range(GROUPS):
        plane_sent(g)
    total = chip(OWN)
    for side, m in ((0, 1), (1, 1), (0, 2), (1, 2), (0, 3), (0, 5), (1, 5)):
        d_copy(side, m).wait_recv()
        total += zr[slot(side, m)].astype(F32)
    last = jnp.where(c == 0, total[8:12], total[12:16])
    out = jnp.concatenate([total[0:8], last], axis=0) + b_out[...].reshape(1, -1)
    o_ref[...] = out.astype(BF16)
    d_sent()


def on_device(tokens, w_in, b_in, w_out, b_out):
    width, hidden = w_in.shape
    half = hidden // 2
    vmem = pl.BlockSpec(memory_space=pltpu.VMEM)
    hbm = pl.BlockSpec(memory_space=pltpu.HBM)
    dma = pltpu.SemaphoreType.DMA
    return pl.pallas_call(
        kernel,
        out_shape=jax.ShapeDtypeStruct(tokens.shape, BF16),
        in_specs=[hbm] * 5,
        out_specs=vmem,
        scratch_shapes=[
            pltpu.VMEM(tokens.shape, BF16),
            pltpu.VMEM((width, hidden), BF16),
            pltpu.VMEM(b_in.shape, F32),
            pltpu.VMEM((hidden, width), BF16),
            pltpu.VMEM(b_out.shape, F32),
            pltpu.VMEM((2, 16, 16, width), BF16),
            pltpu.VMEM((384, width), BF16),
            pltpu.VMEM((GROUPS, 8, 2, 16, half), F32),
            pltpu.VMEM((GROUPS, 8, 2, 16, half), BF16),
            pltpu.VMEM((GROUPS, 16, 16, half), BF16),
            pltpu.VMEM((GROUPS, 8, 2, 16, half), BF16),
            pltpu.VMEM((384, width), F32),
            pltpu.VMEM((16, 16, width), BF16),
            pltpu.VMEM((16, 16, width), BF16),
            pltpu.VMEM((16, 16, width), BF16),
            pltpu.VMEM((16, 16, width), BF16),
            dma((5,)),
            dma((1,)), dma((2, 9)),
            dma((1,)), dma((GROUPS,)),
            dma((GROUPS,)), dma((GROUPS,)),
            dma((GROUPS,)), dma((GROUPS,)),
            dma((1,)), dma((GROUPS,)),
            dma((1,)), dma((2, 9)),
        ],
        compiler_params=pltpu.CompilerParams(
            collective_id=0, has_side_effects=True, vmem_limit_bytes=60 * 2**20
        ),
        cost_estimate=pl.CostEstimate(
            flops=4 * 384 * width * hidden, bytes_accessed=4 * width * hidden, transcendentals=384 * hidden // 16
        ),
    )(tokens, w_in, b_in, w_out, b_out)


def solution(mesh):
    return jax.shard_map(
        on_device,
        mesh=mesh,
        in_specs=(P("row", "col"), P("col", "row"), P("row"), P("row", "col"), P("col")),
        out_specs=P("row", "col"),
        check_vma=False,
    )
```

time: 74.6 us -> 64.2 us (0.86)
  the two profiles are of different devices: /device:TPU:6 before, /device:TPU:1 now
where the time goes in v2:
time: 64.2 us; the launch traced here: 64 us
  Pallas kernels  62.6 us (98%)
  local copies, waits for them, and re-layouts  1.36 us (2%)
    pallas_call x1, Pallas kernels, on_device(): pl.pallas_call(kernel, out_shape=jax.ShapeDtypeStruct(tokens.shape, BF16)...  62.6 us
    unnamed x1, local copies, waits for them, and re-layouts  1.36 us

profile of v2, /device:TPU:1, one launch (start us, length us, event | category | flops | bytes accessed | tf_op | source)
XLA Modules:
  0.0 64.0 jit_solution(8554782396156663372)
XLA Ops:
  0.0 62.6 %shard_map.55 = bf16[12,896]{1,0:T(8,128)(2,1)} custom-call(bf16[12,896]{1,0:T(8,128)(2,1)} %tok_hbm.1, bf16[896,1280]{1,0:T(8,128)(2,1)} %win_ref.1, f32[1280]{0:T(1024)} %bin_hbm.1, bf16[1280,896]{1,0:T(8,128)(2,1)} %wout_ref.1, f32[896]{0:T(1024)} %bout_hbm.1), custom_call_target="tpu_custom_call" | custom-call | flops 1761607680 | bytes 4587520 | tf_op jit(solution)/shard_map/pallas_call | solution.py:307
  62.6 1.4 %copy.7 = bf16[12,896]{1,0:T(8,128)(2,1)} copy(bf16[12,896]{1,0:T(8,128)(2,1)} %shard_map.55) | data formatting | bytes 43008

commit v3 on v2

--- a/solution.py
+++ b/solution.py
@@ -10,21 +10,18 @@
 BF16 = jnp.bfloat16
 F32 = jnp.float32
 PARENT = {1: 0, 2: 0, 5: 0, 3: 2, 4: 5, 6: 5, 7: 5, 8: 5}
-OWN = 15
+PARENT_OUT = {1: 0, 2: 0, 3: 0, 4: 0, 5: 0, 6: 5, 7: 5, 8: 5}
+OWN = 9
 PLANE = [(dy, dx) for dy in (2, 1, 3, 0) for dx in (2, 1, 3, 0) if (dy, dx) != (0, 0)]
 GROUPS = 3
 A_CUTS = (0, 6, 10, 16)
-D_CUTS = (0, 5, 10, 16)
+D_CUTS = (0, 5, 11, 16)
 
 
 def slot(side, m):
-    if m == 3:
-        return 10 - side
-    return {8: 0, 7: 1, 6: 3, 4: 5, 5: 7, 2: 11, 1: 13}[m] + side
-
-
-def parent_out(side, m):
-    return 0 if m == 3 and side == 0 else PARENT[m]
+    if m == 2:
+        return 11 - side
+    return {8: 0, 7: 1, 6: 3, 4: 5, 3: 7, 1: 12, 5: 14}[m] + side
 
 
 def kernel(
@@ -66,7 +63,7 @@
     load_tok.start()
 
     barrier = pltpu.get_barrier_semaphore()
-    peers = [z_peer(dz) for dz in (5, -5, 3, -3, 2, -2, 1, -1)]
+    peers = [z_peer(dz) for dz in (5, -5, 4, -4, 3, -3, 2, -2, 1, -1)]
     peers += [plane_peer(dy, dx) for dy, dx in PLANE] + [sibling]
     for peer in peers:
         pl.semaphore_signal(barrier, inc=1, device_id=peer, device_id_type=pl.DeviceIdType.MESH)
@@ -189,7 +186,7 @@
         return share(k, c) + sr[k].astype(F32)
 
     def d_copy(side, m):
-        dz = (1 - 2 * side) * (m - parent_out(side, m))
+        dz = (1 - 2 * side) * (m - PARENT_OUT[m])
         place = slot(side, m)
         return remote(zs.at[place], zr.at[place], d_send.at[0], d_recv.at[side, m], z_peer(dz))
 
@@ -216,7 +213,7 @@
     for m in (5, 2, 1):
         for side in (0, 1):
             start(a_copy(side, m, OWN))
-    a_sibling(2, OWN)
+    a_sibling(1, OWN)
     for side in (0, 1):
         a_take(side, 2)
         start(a_copy(side, 3, slot(side, 2)))
@@ -227,7 +224,6 @@
         for m in (7, 6, 4):
             start(a_copy(side, m, slot(side, 5)))
     start(a_copy8())
-    a_take(0, 3)
     load_in.wait()
     load_b_in.wait()
     load_b_out.wait()
@@ -235,14 +231,15 @@
     assemble(2)
     project_in(2)
     b_start(2)
-    for m in (6, 7):
+    for m in (3, 6, 7):
         for side in (0, 1):
             a_take(side, m)
     a_copy8().wait_recv()
     a_sibling(0, 0)
-    a_take(0, 4)
-    a_take(1, 4)
-    a_take(1, 3)
+    for side in (0, 1):
+        a_take(side, 4)
+    b_finish(2)
+    c_start(2)
     a_sibling_wait(0)
     assemble(0)
     project_in(0)
@@ -252,13 +249,18 @@
     project_in(1)
     b_start(1)
     load_out.wait()
-    b_finish(2)
+    a_sent()
+    c_wait(2)
+    project_out(2)
+    d_sibling_start(2)
     b_finish(0)
     c_start(0)
-    a_sent()
+    d_sibling(2).wait_recv()
+    for side in (0, 1):
+        d_send_on(side, 1)
+    d_send_on(0, 2)
     b_finish(1)
     c_start(1)
-    c_start(2)
     c_wait(0)
     project_out(0)
     d_sibling_start(0)
@@ -271,27 +273,20 @@
     c_wait(1)
     project_out(1)
     d_sibling_start(1)
-    d_sibling(1).wait_recv()
-    for side in (0, 1):
-        d_send_on(side, 4)
-    d_send_on(1, 3)
-    c_wait(2)
-    project_out(2)
-    d_sibling_start(2)
-    d_send_on(1 - c, 5, (4, 6, 7))
-    d_send_on(c, 5, (4, 6, 7, 8))
-    d_sibling(2).wait_recv()
-    d_send_on(0, 3)
-    d_send_on(0, 2)
-    d_send_on(1, 2, (3,))
-    for side in (0, 1):
-        d_send_on(side, 1)
     for g in range(GROUPS):
         plane_sent(g)
+    d_sibling(1).wait_recv()
+    for m in (4, 3):
+        for side in (0, 1):
+            d_send_on(side, m)
+    d_send_on(1, 2)
+    d_send_on(1 - c, 5, (6, 7))
+    d_send_on(c, 5, (6, 7, 8))
     total = chip(OWN)
-    for side, m in ((0, 1), (1, 1), (0, 2), (1, 2), (0, 3), (0, 5), (1, 5)):
-        d_copy(side, m).wait_recv()
-        total += zr[slot(side, m)].astype(F32)
+    for m in (1, 2, 3, 4, 5):
+        for side in (0, 1):
+            d_copy(side, m).wait_recv()
+            total += zr[slot(side, m)].astype(F32)
     last = jnp.where(c == 0, total[8:12], total[12:16])
     out = jnp.concatenate([total[0:8], last], axis=0) + b_out[...].reshape(1, -1)
     o_ref[...] = out.astype(BF16)

time: 64.2 us -> 67.8 us (1.056)
  Pallas kernels: 62.6 us -> 66.3 us
    pallas_call x1, Pallas kernels: 62.6 us -> 66.3 us  [on_device(): pl.pallas_call(kernel, out_shape=jax.ShapeDtypeStruct(tokens.shape, BF16)...]
where the time goes in v3:
time: 67.8 us; the launch traced here: 67.6 us
  Pallas kernels  66.3 us (98%)
  local copies, waits for them, and re-layouts  1.36 us (2%)
    pallas_call x1, Pallas kernels, on_device(): pl.pallas_call(kernel, out_shape=jax.ShapeDtypeStruct(tokens.shape, BF16)...  66.3 us
    unnamed x1, local copies, waits for them, and re-layouts  1.36 us

profile of v3, /device:TPU:1, one launch (start us, length us, event | category | flops | bytes accessed | tf_op | source)
XLA Modules:
  0.0 67.6 jit_solution(1839141854459742211)
XLA Ops:
  0.0 66.3 %shard_map.55 = bf16[12,896]{1,0:T(8,128)(2,1)} custom-call(bf16[12,896]{1,0:T(8,128)(2,1)} %tok_hbm.1, bf16[896,1280]{1,0:T(8,128)(2,1)} %win_ref.1, f32[1280]{0:T(1024)} %bin_hbm.1, bf16[1280,896]{1,0:T(8,128)(2,1)} %wout_ref.1, f32[896]{0:T(1024)} %bout_hbm.1), custom_call_target="tpu_custom_call" | custom-call | flops 1761607680 | bytes 4587520 | tf_op jit(solution)/shard_map/pallas_call | solution.py:302
  66.3 1.4 %copy.7 = bf16[12,896]{1,0:T(8,128)(2,1)} copy(bf16[12,896]{1,0:T(8,128)(2,1)} %shard_map.55) | data formatting | bytes 43008

commit v4 on v3

--- a/solution.py
+++ b/solution.py
@@ -11,17 +11,24 @@
 F32 = jnp.float32
 PARENT = {1: 0, 2: 0, 5: 0, 3: 2, 4: 5, 6: 5, 7: 5, 8: 5}
 PARENT_OUT = {1: 0, 2: 0, 3: 0, 4: 0, 5: 0, 6: 5, 7: 5, 8: 5}
-OWN = 9
+SPLIT, OWN = 10, 11
 PLANE = [(dy, dx) for dy in (2, 1, 3, 0) for dx in (2, 1, 3, 0) if (dy, dx) != (0, 0)]
 GROUPS = 3
-A_CUTS = (0, 6, 10, 16)
-D_CUTS = (0, 5, 11, 16)
+CHUNKS = ((0, 5), (5, 10), (11, 16))
+PARTS = ((0, 5), (5, 10), (10, 16))
 
 
 def slot(side, m):
-    if m == 2:
-        return 11 - side
-    return {8: 0, 7: 1, 6: 3, 4: 5, 3: 7, 1: 12, 5: 14}[m] + side
+    if m == 3:
+        return (2, SPLIT)[side]
+    return {5: 0, 4: 3, 8: 5, 7: 6, 6: 8, 1: 12, 2: 14}[m] + side
+
+
+def first_row(place):
+    if not isinstance(place, int):
+        return 24 * place
+    group = 0 if place < 5 else 1 if place < 10 else 2
+    return 128 * group + 24 * (place - CHUNKS[group][0])
 
 
 def kernel(
@@ -85,12 +92,12 @@
 
     def a_copy(side, m, at):
         sign = 1 - 2 * side
-        dz = -sign * (m - PARENT[m])
+        dz = -sign * (m - (0 if m == 3 and side == 1 else PARENT[m]))
         place = slot(side, m)
         return remote(ta.at[c, at], ta.at[c, place], a_send.at[0], a_recv.at[side, m], z_peer(dz))
 
     def a_copy8():
-        return remote(ta.at[c, slot(0, 5) + c], ta.at[c, 0], a_send.at[0], a_recv.at[0, 8], z_peer(-3 * s8))
+        return remote(ta.at[c, slot(0, 5) + c], ta.at[c, slot(0, 8)], a_send.at[0], a_recv.at[0, 8], z_peer(-3 * s8))
 
     def a_wait(side, m):
         a_copy(side, m, 0).wait_recv()
@@ -99,25 +106,28 @@
         start(remote(ta.at[c, place], ta.at[c, place], as_send.at[0], as_recv.at[g], sibling))
 
     def a_sibling_wait(g):
-        part = pl.ds(A_CUTS[g], A_CUTS[g + 1] - A_CUTS[g])
+        part = pl.ds(PARTS[g][0], PARTS[g][1] - PARTS[g][0])
         all_of(ta.at[1 - c, part], as_send.at[0], as_recv.at[g]).wait_recv()
 
     def a_take(side, m):
         a_wait(side, m)
         place = slot(side, m)
-        a_sibling(sum(place >= cut for cut in A_CUTS[1:]), place)
+        a_sibling(0 if place < 5 else 1 if place < 10 else 2, place)
 
     def a_sent():
         all_of(ta.at[c, pl.ds(0, 15)], a_send.at[0], as_recv.at[0]).wait_send()
         all_of(ta.at[c], as_send.at[0], as_recv.at[0]).wait_send()
 
     def assemble(g):
-        for k in range(A_CUTS[g], A_CUTS[g + 1], 2):
-            rows = []
-            for i in (k, k + 1):
-                first, second = ta[0, i].astype(F32), ta[1, i].astype(F32)
-                rows += [first[0:8], second[0:8], first[8:16] + second[8:16]]
-            xs[24 * k : 24 * k + 48, :] = jnp.concatenate(rows, axis=0).astype(BF16)
+        rows = []
+        for k in range(*CHUNKS[g]):
+            first, second = ta[0, k].astype(F32), ta[1, k].astype(F32)
+            rows += [first[0:8], second[0:8], first[8:16] + second[8:16]]
+        if g < 2:
+            rows.append(ta[g, SPLIT].astype(F32)[0:8])
+        else:
+            rows.append(ta[0, SPLIT].astype(F32)[8:16] + ta[1, SPLIT].astype(F32)[8:16])
+        xs[128 * g : 128 * g + 128, :] = jnp.concatenate(rows, axis=0).astype(BF16)
 
     def project_in(g):
         lhs = xs[128 * g : 128 * g + 128, :]
@@ -170,15 +180,19 @@
         po[128 * g : 128 * g + 128, :] = total
 
     def share(k, core):
-        first = po[pl.ds(pl.multiple_of(24 * k + 8 * core, 8), 8), :]
-        return jnp.concatenate([first, po[pl.ds(pl.multiple_of(24 * k + 16, 8), 8), :]], axis=0)
+        if isinstance(k, int) and k == SPLIT:
+            first, rest = 128 * core + 120, 256 + 120
+        else:
+            first, rest = first_row(k) + 8 * core, first_row(k) + 16
+        first, rest = (po[pl.ds(pl.multiple_of(at, 8), 8), :] for at in (first, rest))
+        return jnp.concatenate([first, rest], axis=0)
 
     def d_sibling(g):
-        part = pl.ds(D_CUTS[g], D_CUTS[g + 1] - D_CUTS[g])
+        part = pl.ds(PARTS[g][0], PARTS[g][1] - PARTS[g][0])
         return remote(ss.at[part], sr.at[part], ds_send.at[0], ds_recv.at[g], sibling)
 
     def d_sibling_start(g):
-        for k in range(D_CUTS[g], D_CUTS[g + 1]):
+        for k in range(*PARTS[g]):
             ss[k] = share(k, 1 - c).astype(BF16)
         start(d_sibling(g))
 
@@ -191,7 +205,7 @@
         return remote(zs.at[place], zr.at[place], d_send.at[0], d_recv.at[side, m], z_peer(dz))
 
     def d_copy8():
-        return remote(zs.at[0], zr.at[0], d_send.at[0], d_recv.at[0, 8], z_peer(3 * s8))
+        return remote(zs.at[slot(0, 8)], zr.at[slot(0, 8)], d_send.at[0], d_recv.at[0, 8], z_peer(3 * s8))
 
     def d_sent():
         all_of(sr, ds_send.at[0], ds_recv.at[0]).wait_send()
@@ -203,27 +217,25 @@
         for n in below:
             if n == 8:
                 d_copy8().wait_recv()
-                total += zr[0].astype(F32)
+                total += zr[slot(0, 8)].astype(F32)
             else:
                 d_copy(side, n).wait_recv()
                 total += zr[slot(side, n)].astype(F32)
         zs[place] = total.astype(BF16)
         start(d_copy(side, m))
 
-    for m in (5, 2, 1):
+    a_sibling(2, OWN)
+    for m in (1, 2):
         for side in (0, 1):
             start(a_copy(side, m, OWN))
-    a_sibling(1, OWN)
+    start(a_copy(1, 3, OWN))
     for side in (0, 1):
-        a_take(side, 2)
-        start(a_copy(side, 3, slot(side, 2)))
-    for side in (0, 1):
-        a_take(side, 1)
-    for side in (0, 1):
-        a_take(side, 5)
-        for m in (7, 6, 4):
-            start(a_copy(side, m, slot(side, 5)))
-    start(a_copy8())
+        start(a_copy(side, 5, OWN))
+    for m in (1, 2):
+        for side in (0, 1):
+            a_take(side, m)
+    start(a_copy(0, 3, slot(0, 2)))
+    a_take(1, 3)
     load_in.wait()
     load_b_in.wait()
     load_b_out.wait()
@@ -231,55 +243,61 @@
     assemble(2)
     project_in(2)
     b_start(2)
-    for m in (3, 6, 7):
-        for side in (0, 1):
-            a_take(side, m)
-    a_copy8().wait_recv()
-    a_sibling(0, 0)
+    for side in (0, 1):
+        a_take(side, 5)
+        for m in (4, 7, 6):
+            start(a_copy(side, m, slot(side, 5)))
+    start(a_copy8())
+    a_take(0, 3)
     for side in (0, 1):
         a_take(side, 4)
-    b_finish(2)
-    c_start(2)
     a_sibling_wait(0)
     assemble(0)
     project_in(0)
     b_start(0)
+    for m in (6, 7):
+        for side in (0, 1):
+            a_take(side, m)
+    a_copy8().wait_recv()
+    a_sibling(1, slot(0, 8))
     a_sibling_wait(1)
     assemble(1)
     project_in(1)
     b_start(1)
     load_out.wait()
     a_sent()
-    c_wait(2)
-    project_out(2)
-    d_sibling_start(2)
+    b_finish(2)
     b_finish(0)
     c_start(0)
-    d_sibling(2).wait_recv()
-    for side in (0, 1):
-        d_send_on(side, 1)
-    d_send_on(0, 2)
     b_finish(1)
     c_start(1)
     c_wait(0)
     project_out(0)
     d_sibling_start(0)
+    c_start(2)
     d_sibling(0).wait_recv()
-    zs[0] = chip(0).astype(BF16)
-    start(d_copy8())
-    for m in (7, 6):
-        for side in (0, 1):
-            d_send_on(side, m)
+    for side in (0, 1):
+        d_send_on(side, 4)
+    d_send_on(0, 3)
     c_wait(1)
     project_out(1)
     d_sibling_start(1)
+    d_sibling(1).wait_recv()
+    zs[slot(0, 8)] = chip(slot(0, 8)).astype(BF16)
+    start(d_copy8())
+    for m in (7, 6):
+        for side in (0, 1):
+            d_send_on(side, m)
+    c_wait(2)
+    project_out(2)
+    d_sibling_start(2)
     for g in range(GROUPS):
         plane_sent(g)
-    d_sibling(1).wait_recv()
-    for m in (4, 3):
+    d_sibling(2).wait_recv()
+    for m in (2, 1):
         for side in (0, 1):
             d_send_on(side, m)
-    d_send_on(1, 2)
+    d_send_on(1, 3)
     d_send_on(1 - c, 5, (6, 7))
     d_send_on(c, 5, (6, 7, 8))
     total = chip(OWN)

time: 67.8 us -> 67.9 us (level)
  no operation moved by 1% of the time
where the time goes in v4:
time: 67.9 us; the launch traced here: 67.7 us
  Pallas kernels  66.4 us (98%)
  local copies, waits for them, and re-layouts  1.36 us (2%)
    pallas_call x1, Pallas kernels, on_device(): pl.pallas_call(kernel, out_shape=jax.ShapeDtypeStruct(tokens.shape, BF16)...  66.4 us
    unnamed x1, local copies, waits for them, and re-layouts  1.36 us

profile of v4, /device:TPU:1, one launch (start us, length us, event | category | flops | bytes accessed | tf_op | source)
XLA Modules:
  0.0 67.7 jit_solution(544813472681015391)
XLA Ops:
  0.0 66.4 %shard_map.55 = bf16[12,896]{1,0:T(8,128)(2,1)} custom-call(bf16[12,896]{1,0:T(8,128)(2,1)} %tok_hbm.1, bf16[896,1280]{1,0:T(8,128)(2,1)} %win_ref.1, f32[1280]{0:T(1024)} %bin_hbm.1, bf16[1280,896]{1,0:T(8,128)(2,1)} %wout_ref.1, f32[896]{0:T(1024)} %bout_hbm.1), custom_call_target="tpu_custom_call" | custom-call | flops 1761607680 | bytes 4587520 | tf_op jit(solution)/shard_map/pallas_call | solution.py:320
  66.4 1.4 %copy.7 = bf16[12,896]{1,0:T(8,128)(2,1)} copy(bf16[12,896]{1,0:T(8,128)(2,1)} %shard_map.55) | data formatting | bytes 43008

commit v5 on v4

--- a/solution.py
+++ b/solution.py
@@ -22,6 +22,32 @@
     if m == 3:
         return (2, SPLIT)[side]
     return {5: 0, 4: 3, 8: 5, 7: 6, 6: 8, 1: 12, 2: 14}[m] + side
+
+
+def pack(first, last):
+    tiles = first.shape[1] // 128
+    groups = [first[:, 128 * t : 128 * t + 128] for t in range(tiles)]
+    ends = [last[:, 128 * t : 128 * t + 128] for t in range(tiles)]
+    if tiles % 2:
+        ends.append(jnp.zeros_like(ends[0]))
+    groups += [jnp.concatenate(ends[t : t + 2], axis=0) for t in range(0, len(ends), 2)]
+    if len(groups) % 2:
+        groups.append(jnp.zeros_like(groups[0]))
+    return jnp.concatenate(groups, axis=0)
+
+
+def packed_rows(tiles):
+    groups = tiles + (tiles + 1) // 2
+    return 8 * (groups + groups % 2)
+
+
+def first_of(packed, t):
+    return packed[8 * t : 8 * t + 8]
+
+
+def last_of(packed, t, tiles):
+    at = 8 * (tiles + t // 2) + 4 * (t % 2)
+    return packed[at : at + 4]
 
 
 def first_row(place):
@@ -41,6 +67,7 @@
     z, c = row // 2, row % 2
     y, x = col // 4, col % 4
     half = pb.shape[-1]
+    tiles = xs.shape[1] // 128
     s8 = 1 - 2 * c
 
     def z_peer(dz):
@@ -83,11 +110,7 @@
     load_tok.wait()
 
     own = tok[...].astype(F32)
-    tail, none = own[8:12], jnp.zeros((4, own.shape[1]), F32)
-    tail = jnp.where(
-        c == 0, jnp.concatenate([tail, none], axis=0), jnp.concatenate([none, tail], axis=0)
-    )
-    ta[c, OWN] = jnp.concatenate([own[0:8], tail], axis=0).astype(BF16)
+    ta[c, OWN] = pack(own[0:8], own[8:12]).astype(BF16)
     pl.semaphore_wait(barrier, len(peers))
 
     def a_copy(side, m, at):
@@ -119,15 +142,14 @@
         all_of(ta.at[c], as_send.at[0], as_recv.at[0]).wait_send()
 
     def assemble(g):
-        rows = []
-        for k in range(*CHUNKS[g]):
-            first, second = ta[0, k].astype(F32), ta[1, k].astype(F32)
-            rows += [first[0:8], second[0:8], first[8:16] + second[8:16]]
-        if g < 2:
-            rows.append(ta[g, SPLIT].astype(F32)[0:8])
-        else:
-            rows.append(ta[0, SPLIT].astype(F32)[8:16] + ta[1, SPLIT].astype(F32)[8:16])
-        xs[128 * g : 128 * g + 128, :] = jnp.concatenate(rows, axis=0).astype(BF16)
+        chunks = [(ta[0, k].astype(F32), ta[1, k].astype(F32)) for k in (*range(*CHUNKS[g]), SPLIT)]
+        for t in range(tiles):
+            rows = []
+            for first, second in chunks:
+                rows += [first_of(first, t), first_of(second, t)]
+                rows += [last_of(first, t, tiles), last_of(second, t, tiles)]
+            rows[-4:] = (rows[-4:-3], rows[-3:-2], rows[-2:])[g]
+            xs[128 * g : 128 * g + 128, 128 * t : 128 * t + 128] = jnp.concatenate(rows, axis=0).astype(BF16)
 
     def project_in(g):
         lhs = xs[128 * g : 128 * g + 128, :]
@@ -185,14 +207,21 @@
         else:
             first, rest = first_row(k) + 8 * core, first_row(k) + 16
         first, rest = (po[pl.ds(pl.multiple_of(at, 8), 8), :] for at in (first, rest))
-        return jnp.concatenate([first, rest], axis=0)
+        return pack(first, jnp.where(core == 0, rest[0:4], rest[4:8]))
+
+    def d_sibling_one(k):
+        return remote(ss.at[k], sr.at[k], ds_send.at[0], ds_recv.at[k], sibling)
+
+    def d_sibling_start_one(k):
+        ss[k] = share(k, 1 - c).astype(BF16)
+        start(d_sibling_one(k))
 
     def d_sibling(g):
-        part = pl.ds(PARTS[g][0], PARTS[g][1] - PARTS[g][0])
-        return remote(ss.at[part], sr.at[part], ds_send.at[0], ds_recv.at[g], sibling)
+        part = pl.ds(CHUNKS[g][0], 5)
+        return remote(ss.at[part], sr.at[part], ds_send.at[0], ds_recv.at[CHUNKS[g][0]], sibling)
 
     def d_sibling_start(g):
-        for k in range(*PARTS[g]):
+        for k in range(*CHUNKS[g]):
             ss[k] = share(k, 1 - c).astype(BF16)
         start(d_sibling(g))
 
@@ -224,18 +253,25 @@
         zs[place] = total.astype(BF16)
         start(d_copy(side, m))
 
+    for m in (5, 1, 2):
+        for side in (0, 1):
+            start(a_copy(side, m, OWN))
+    start(a_copy(1, 3, OWN))
     a_sibling(2, OWN)
     for m in (1, 2):
         for side in (0, 1):
-            start(a_copy(side, m, OWN))
-    start(a_copy(1, 3, OWN))
-    for side in (0, 1):
-        start(a_copy(side, 5, OWN))
-    for m in (1, 2):
-        for side in (0, 1):
             a_take(side, m)
     start(a_copy(0, 3, slot(0, 2)))
+    for side in (0, 1):
+        a_wait(side, 5)
+        start(a_copy(side, 4, slot(side, 5)))
+    start(a_copy8())
+    for m in (7, 6):
+        for side in (0, 1):
+            start(a_copy(side, m, slot(side, 5)))
     a_take(1, 3)
+    for side in (0, 1):
+        a_sibling(0, slot(side, 5))
     load_in.wait()
     load_b_in.wait()
     load_b_out.wait()
@@ -243,11 +279,6 @@
     assemble(2)
     project_in(2)
     b_start(2)
-    for side in (0, 1):
-        a_take(side, 5)
-        for m in (4, 7, 6):
-            start(a_copy(side, m, slot(side, 5)))
-    start(a_copy8())
     a_take(0, 3)
     for side in (0, 1):
         a_take(side, 4)
@@ -281,32 +312,37 @@
     d_send_on(0, 3)
     c_wait(1)
     project_out(1)
-    d_sibling_start(1)
-    d_sibling(1).wait_recv()
+    for k in (slot(0, 8), slot(0, 7), slot(1, 7), slot(0, 6), slot(1, 6)):
+        d_sibling_start_one(k)
+    d_sibling_one(slot(0, 8)).wait_recv()
     zs[slot(0, 8)] = chip(slot(0, 8)).astype(BF16)
     start(d_copy8())
     for m in (7, 6):
         for side in (0, 1):
+            d_sibling_one(slot(side, m)).wait_recv()
             d_send_on(side, m)
     c_wait(2)
     project_out(2)
+    d_sibling_start_one(SPLIT)
     d_sibling_start(2)
+    d_send_on(1 - c, 5, (6, 7))
+    d_send_on(c, 5, (6, 7, 8))
+    d_sibling_one(SPLIT).wait_recv()
+    d_send_on(1, 3)
+    d_sibling(2).wait_recv()
+    for m in (2, 1):
+        for side in (0, 1):
+            d_send_on(side, m)
     for g in range(GROUPS):
         plane_sent(g)
-    d_sibling(2).wait_recv()
-    for m in (2, 1):
-        for side in (0, 1):
-            d_send_on(side, m)
-    d_send_on(1, 3)
-    d_send_on(1 - c, 5, (6, 7))
-    d_send_on(c, 5, (6, 7, 8))
     total = chip(OWN)
     for m in (1, 2, 3, 4, 5):
         for side in (0, 1):
             d_copy(side, m).wait_recv()
             total += zr[slot(side, m)].astype(F32)
-    last = jnp.where(c == 0, total[8:12], total[12:16])
-    out = jnp.concatenate([total[0:8], last], axis=0) + b_out[...].reshape(1, -1)
+    first = jnp.concatenate([first_of(total, t) for t in range(tiles)], axis=1)
+    last = jnp.concatenate([last_of(total, t, tiles) for t in range(tiles)], axis=1)
+    out = jnp.concatenate([first, last], axis=0) + b_out[...].reshape(1, -1)
     o_ref[...] = out.astype(BF16)
     d_sent()
 
@@ -314,6 +350,7 @@
 def on_device(tokens, w_in, b_in, w_out, b_out):
     width, hidden = w_in.shape
     half = hidden // 2
+    chunk = packed_rows(width // 128)
     vmem = pl.BlockSpec(memory_space=pltpu.VMEM)
     hbm = pl.BlockSpec(memory_space=pltpu.HBM)
     dma = pltpu.SemaphoreType.DMA
@@ -328,23 +365,23 @@
             pltpu.VMEM(b_in.shape, F32),
             pltpu.VMEM((hidden, width), BF16),
             pltpu.VMEM(b_out.shape, F32),
-            pltpu.VMEM((2, 16, 16, width), BF16),
+            pltpu.VMEM((2, 16, chunk, 128), BF16),
             pltpu.VMEM((384, width), BF16),
             pltpu.VMEM((GROUPS, 8, 2, 16, half), F32),
             pltpu.VMEM((GROUPS, 8, 2, 16, half), BF16),
             pltpu.VMEM((GROUPS, 16, 16, half), BF16),
             pltpu.VMEM((GROUPS, 8, 2, 16, half), BF16),
             pltpu.VMEM((384, width), F32),
-            pltpu.VMEM((16, 16, width), BF16),
-            pltpu.VMEM((16, 16, width), BF16),
-            pltpu.VMEM((16, 16, width), BF16),
-            pltpu.VMEM((16, 16, width), BF16),
+            pltpu.VMEM((16, chunk, 128), BF16),
+            pltpu.VMEM((16, chunk, 128), BF16),
+            pltpu.VMEM((16, chunk, 128), BF16),
+            pltpu.VMEM((16, chunk, 128), BF16),
             dma((5,)),
             dma((1,)), dma((2, 9)),
             dma((1,)), dma((GROUPS,)),
             dma((GROUPS,)), dma((GROUPS,)),
             dma((GROUPS,)), dma((GROUPS,)),
-            dma((1,)), dma((GROUPS,)),
+            dma((1,)), dma((16,)),
             dma((1,)), dma((2, 9)),
         ],
         compiler_params=pltpu.CompilerParams(

time: 67.9 us -> 63.4 us (0.934)
  Pallas kernels: 66.4 us -> 61.8 us
    pallas_call x1, Pallas kernels: 66.4 us -> 61.8 us  [on_device(): pl.pallas_call(kernel, out_shape=jax.ShapeDtypeStruct(tokens.shape, BF16)...]
where the time goes in v5:
time: 63.4 us; the launch traced here: 63.2 us
  Pallas kernels  61.8 us (97%)
  local copies, waits for them, and re-layouts  1.36 us (2%)
    pallas_call x1, Pallas kernels, on_device(): pl.pallas_call(kernel, out_shape=jax.ShapeDtypeStruct(tokens.shape, BF16)...  61.8 us
    unnamed x1, local copies, waits for them, and re-layouts  1.36 us

profile of v5, /device:TPU:1, one launch (start us, length us, event | category | flops | bytes accessed | tf_op | source)
XLA Modules:
  0.0 63.2 jit_solution(5638283378681786032)
XLA Ops:
  0.0 61.8 %shard_map.55 = bf16[12,896]{1,0:T(8,128)(2,1)} custom-call(bf16[12,896]{1,0:T(8,128)(2,1)} %tok_hbm.1, bf16[896,1280]{1,0:T(8,128)(2,1)} %win_ref.1, f32[1280]{0:T(1024)} %bin_hbm.1, bf16[1280,896]{1,0:T(8,128)(2,1)} %wout_ref.1, f32[896]{0:T(1024)} %bout_hbm.1), custom_call_target="tpu_custom_call" | custom-call | flops 1761607680 | bytes 4587520 | tf_op jit(solution)/shard_map/pallas_call | solution.py:357
  61.8 1.4 %copy.7 = bf16[12,896]{1,0:T(8,128)(2,1)} copy(bf16[12,896]{1,0:T(8,128)(2,1)} %shard_map.55) | data formatting | bytes 43008

commit v6 on v5

--- a/solution.py
+++ b/solution.py
@@ -10,7 +10,7 @@
 BF16 = jnp.bfloat16
 F32 = jnp.float32
 PARENT = {1: 0, 2: 0, 5: 0, 3: 2, 4: 5, 6: 5, 7: 5, 8: 5}
-PARENT_OUT = {1: 0, 2: 0, 3: 0, 4: 0, 5: 0, 6: 5, 7: 5, 8: 5}
+PARENT_OUT = {1: 0, 2: 0, 3: 0, 4: 0, 5: 4, 6: 4, 7: 4, 8: 4}
 SPLIT, OWN = 10, 11
 PLANE = [(dy, dx) for dy in (2, 1, 3, 0) for dx in (2, 1, 3, 0) if (dy, dx) != (0, 0)]
 GROUPS = 3
@@ -234,7 +234,7 @@
         return remote(zs.at[place], zr.at[place], d_send.at[0], d_recv.at[side, m], z_peer(dz))
 
     def d_copy8():
-        return remote(zs.at[slot(0, 8)], zr.at[slot(0, 8)], d_send.at[0], d_recv.at[0, 8], z_peer(3 * s8))
+        return remote(zs.at[slot(0, 8)], zr.at[slot(0, 8)], d_send.at[0], d_recv.at[0, 8], z_peer(4 * s8))
 
     def d_sent():
         all_of(sr, ds_send.at[0], ds_recv.at[0]).wait_send()
@@ -264,9 +264,8 @@
     start(a_copy(0, 3, slot(0, 2)))
     for side in (0, 1):
         a_wait(side, 5)
-        start(a_copy(side, 4, slot(side, 5)))
     start(a_copy8())
-    for m in (7, 6):
+    for m in (7, 6, 4):
         for side in (0, 1):
             start(a_copy(side, m, slot(side, 5)))
     a_take(1, 3)
@@ -279,41 +278,34 @@
     assemble(2)
     project_in(2)
     b_start(2)
+    for m in (6, 7):
+        for side in (0, 1):
+            a_take(side, m)
+    a_copy8().wait_recv()
+    a_sibling(1, slot(0, 8))
     a_take(0, 3)
     for side in (0, 1):
         a_take(side, 4)
+    a_sibling_wait(1)
+    assemble(1)
+    project_in(1)
+    b_start(1)
     a_sibling_wait(0)
     assemble(0)
     project_in(0)
     b_start(0)
-    for m in (6, 7):
-        for side in (0, 1):
-            a_take(side, m)
-    a_copy8().wait_recv()
-    a_sibling(1, slot(0, 8))
-    a_sibling_wait(1)
-    assemble(1)
-    project_in(1)
-    b_start(1)
     load_out.wait()
     a_sent()
     b_finish(2)
+    b_finish(1)
+    c_start(1)
     b_finish(0)
     c_start(0)
-    b_finish(1)
-    c_start(1)
-    c_wait(0)
-    project_out(0)
-    d_sibling_start(0)
-    c_start(2)
-    d_sibling(0).wait_recv()
-    for side in (0, 1):
-        d_send_on(side, 4)
-    d_send_on(0, 3)
     c_wait(1)
     project_out(1)
     for k in (slot(0, 8), slot(0, 7), slot(1, 7), slot(0, 6), slot(1, 6)):
         d_sibling_start_one(k)
+    c_start(2)
     d_sibling_one(slot(0, 8)).wait_recv()
     zs[slot(0, 8)] = chip(slot(0, 8)).astype(BF16)
     start(d_copy8())
@@ -321,12 +313,19 @@
         for side in (0, 1):
             d_sibling_one(slot(side, m)).wait_recv()
             d_send_on(side, m)
+    c_wait(0)
+    project_out(0)
+    d_sibling_start(0)
+    d_sibling(0).wait_recv()
+    for side in (0, 1):
+        d_send_on(side, 5)
+    d_send_on(0, 3)
     c_wait(2)
     project_out(2)
     d_sibling_start_one(SPLIT)
     d_sibling_start(2)
-    d_send_on(1 - c, 5, (6, 7))
-    d_send_on(c, 5, (6, 7, 8))
+    d_send_on(1 - c, 4, (5, 6, 7))
+    d_send_on(c, 4, (5, 6, 7, 8))
     d_sibling_one(SPLIT).wait_recv()
     d_send_on(1, 3)
     d_sibling(2).wait_recv()
@@ -336,7 +335,7 @@
     for g in range(GROUPS):
         plane_sent(g)
     total = chip(OWN)
-    for m in (1, 2, 3, 4, 5):
+    for m in (1, 2, 3, 4):
         for side in (0, 1):
             d_copy(side, m).wait_recv()
             total += zr[slot(side, m)].astype(F32)

time: 63.4 us -> 63.7 us (level)
  no operation moved by 1% of the time
where the time goes in v6:
time: 63.7 us; the launch traced here: 63.5 us
  Pallas kernels  62.1 us (97%)
  local copies, waits for them, and re-layouts  1.36 us (2%)
    pallas_call x1, Pallas kernels, on_device(): pl.pallas_call(kernel, out_shape=jax.ShapeDtypeStruct(tokens.shape, BF16)...  62.1 us
    unnamed x1, local copies, waits for them, and re-layouts  1.36 us

profile of v6, /device:TPU:1, one launch (start us, length us, event | category | flops | bytes accessed | tf_op | source)
XLA Modules:
  0.0 63.5 jit_solution(14440636185585338927)
XLA Ops:
  0.0 62.1 %shard_map.55 = bf16[12,896]{1,0:T(8,128)(2,1)} custom-call(bf16[12,896]{1,0:T(8,128)(2,1)} %tok_hbm.1, bf16[896,1280]{1,0:T(8,128)(2,1)} %win_ref.1, f32[1280]{0:T(1024)} %bin_hbm.1, bf16[1280,896]{1,0:T(8,128)(2,1)} %wout_ref.1, f32[896]{0:T(1024)} %bout_hbm.1), custom_call_target="tpu_custom_call" | custom-call | flops 1761607680 | bytes 4587520 | tf_op jit(solution)/shard_map/pallas_call | solution.py:356
  62.1 1.4 %copy.7 = bf16[12,896]{1,0:T(8,128)(2,1)} copy(bf16[12,896]{1,0:T(8,128)(2,1)} %shard_map.55) | data formatting | bytes 43008

commit v7 on v5

--- a/solution.py
+++ b/solution.py
@@ -10,7 +10,7 @@
 BF16 = jnp.bfloat16
 F32 = jnp.float32
 PARENT = {1: 0, 2: 0, 5: 0, 3: 2, 4: 5, 6: 5, 7: 5, 8: 5}
-PARENT_OUT = {1: 0, 2: 0, 3: 0, 4: 0, 5: 0, 6: 5, 7: 5, 8: 5}
+PARENT_OUT = {1: 0, 2: 0, 3: 0, 4: 0, 5: 4, 6: 4, 7: 4, 8: 4}
 SPLIT, OWN = 10, 11
 PLANE = [(dy, dx) for dy in (2, 1, 3, 0) for dx in (2, 1, 3, 0) if (dy, dx) != (0, 0)]
 GROUPS = 3
@@ -234,7 +234,7 @@
         return remote(zs.at[place], zr.at[place], d_send.at[0], d_recv.at[side, m], z_peer(dz))
 
     def d_copy8():
-        return remote(zs.at[slot(0, 8)], zr.at[slot(0, 8)], d_send.at[0], d_recv.at[0, 8], z_peer(3 * s8))
+        return remote(zs.at[slot(0, 8)], zr.at[slot(0, 8)], d_send.at[0], d_recv.at[0, 8], z_peer(4 * s8))
 
     def d_sent():
         all_of(sr, ds_send.at[0], ds_recv.at[0]).wait_send()
@@ -308,7 +308,7 @@
     c_start(2)
     d_sibling(0).wait_recv()
     for side in (0, 1):
-        d_send_on(side, 4)
+        d_send_on(side, 5)
     d_send_on(0, 3)
     c_wait(1)
     project_out(1)
@@ -325,8 +325,8 @@
     project_out(2)
     d_sibling_start_one(SPLIT)
     d_sibling_start(2)
-    d_send_on(1 - c, 5, (6, 7))
-    d_send_on(c, 5, (6, 7, 8))
+    d_send_on(1 - c, 4, (5, 6, 7))
+    d_send_on(c, 4, (5, 6, 7, 8))
     d_sibling_one(SPLIT).wait_recv()
     d_send_on(1, 3)
     d_sibling(2).wait_recv()
@@ -336,7 +336,7 @@
     for g in range(GROUPS):
         plane_sent(g)
     total = chip(OWN)
-    for m in (1, 2, 3, 4, 5):
+    for m in (1, 2, 3, 4):
         for side in (0, 1):
             d_copy(side, m).wait_recv()
             total += zr[slot(side, m)].astype(F32)

time: 63.4 us -> 64.2 us (1.013)
  Pallas kernels: 61.8 us -> 62.6 us
    pallas_call x1, Pallas kernels: 61.8 us -> 62.6 us  [on_device(): pl.pallas_call(kernel, out_shape=jax.ShapeDtypeStruct(tokens.shape, BF16)...]
where the time goes in v7:
time: 64.2 us; the launch traced here: 64 us
  Pallas kernels  62.6 us (98%)
  local copies, waits for them, and re-layouts  1.36 us (2%)
    pallas_call x1, Pallas kernels, on_device(): pl.pallas_call(kernel, out_shape=jax.ShapeDtypeStruct(tokens.shape, BF16)...  62.6 us
    unnamed x1, local copies, waits for them, and re-layouts  1.36 us

profile of v7, /device:TPU:1, one launch (start us, length us, event | category | flops | bytes accessed | tf_op | source)
XLA Modules:
  0.0 64.0 jit_solution(12090063987965146448)
XLA Ops:
  0.0 62.6 %shard_map.55 = bf16[12,896]{1,0:T(8,128)(2,1)} custom-call(bf16[12,896]{1,0:T(8,128)(2,1)} %tok_hbm.1, bf16[896,1280]{1,0:T(8,128)(2,1)} %win_ref.1, f32[1280]{0:T(1024)} %bin_hbm.1, bf16[1280,896]{1,0:T(8,128)(2,1)} %wout_ref.1, f32[896]{0:T(1024)} %bout_hbm.1), custom_call_target="tpu_custom_call" | custom-call | flops 1761607680 | bytes 4587520 | tf_op jit(solution)/shard_map/pallas_call | solution.py:357
  62.6 1.4 %copy.7 = bf16[12,896]{1,0:T(8,128)(2,1)} copy(bf16[12,896]{1,0:T(8,128)(2,1)} %shard_map.55) | data formatting | bytes 43008

commit v8 on v5

--- a/solution.py
+++ b/solution.py
@@ -302,10 +302,10 @@
     c_start(0)
     b_finish(1)
     c_start(1)
+    c_start(2)
     c_wait(0)
     project_out(0)
     d_sibling_start(0)
-    c_start(2)
     d_sibling(0).wait_recv()
     for side in (0, 1):
         d_send_on(side, 4)

time: 63.4 us -> 64.5 us (1.017)
  Pallas kernels: 61.8 us -> 62.9 us
    pallas_call x1, Pallas kernels: 61.8 us -> 62.9 us  [on_device(): pl.pallas_call(kernel, out_shape=jax.ShapeDtypeStruct(tokens.shape, BF16)...]
where the time goes in v8:
time: 64.5 us; the launch traced here: 64.3 us
  Pallas kernels  62.9 us (98%)
  local copies, waits for them, and re-layouts  1.36 us (2%)
    pallas_call x1, Pallas kernels, on_device(): pl.pallas_call(kernel, out_shape=jax.ShapeDtypeStruct(tokens.shape, BF16)...  62.9 us
    unnamed x1, local copies, waits for them, and re-layouts  1.36 us

profile of v8, /device:TPU:1, one launch (start us, length us, event | category | flops | bytes accessed | tf_op | source)
XLA Modules:
  0.0 64.3 jit_solution(13440947304875778512)
XLA Ops:
  0.0 62.9 %shard_map.55 = bf16[12,896]{1,0:T(8,128)(2,1)} custom-call(bf16[12,896]{1,0:T(8,128)(2,1)} %tok_hbm.1, bf16[896,1280]{1,0:T(8,128)(2,1)} %win_ref.1, f32[1280]{0:T(1024)} %bin_hbm.1, bf16[1280,896]{1,0:T(8,128)(2,1)} %wout_ref.1, f32[896]{0:T(1024)} %bout_hbm.1), custom_call_target="tpu_custom_call" | custom-call | flops 1761607680 | bytes 4587520 | tf_op jit(solution)/shard_map/pallas_call | solution.py:357
  62.9 1.4 %copy.7 = bf16[12,896]{1,0:T(8,128)(2,1)} copy(bf16[12,896]{1,0:T(8,128)(2,1)} %shard_map.55) | data formatting | bytes 43008
